TPU v7x, 512 devices: a whole 4x4x16 slice. The times are simulated.
512 devices in a mesh: row: 32 (over x, y, core), tensor: 16 (over z).
Axes of the slice: x: 4, y: 4, z: 16, core: 2. Of those that a mesh axis runs over, the one named last changes fastest.
Arguments:
- ssm_input: bfloat16 [128, 8, 8192], P('row', None, 'tensor'), may hold values from -12 to 12
- gate_input: bfloat16 [128, 8, 8192], P('row', None, 'tensor'), may hold values from -6 to 6
- write_vectors: bfloat16 [128, 8, 4096], P('row', None, 'tensor'), may hold values from -0.375 to 0.375
- read_vectors: bfloat16 [128, 8, 4096], P('row', None, 'tensor'), may hold values from -6 to 6
- step_logit: float32 [128, 8, 128], P('row', None, 'tensor'), may hold values from -4 to 4
- step_bias: float32 [128], P('tensor'), may hold values from -2 to 0.5
- decay_rate: float32 [128], P('tensor'), may hold values from 0.05 to 4
- skip_gain: float32 [128], P('tensor'), may hold values from 0.5 to 1.5
- norm_gain: float32 [8192], P('tensor'), may hold values from 0.1 to 1.9
- ssm_state: bfloat16 [128, 128, 64, 256], P('row', 'tensor'), may hold values from -0.375 to 0.375
- accepted: int32 [128], P('row'), may hold values from 0 to 8
- out_weight: bfloat16 [8192, 8192], P('tensor', 'row'), may hold values from -0.0625 to 0.0625
- token_embeds: bfloat16 [128, 8, 8192], P('tensor', None, 'row'), may hold values from -6 to 6
- feat_weight: bfloat16 [8192, 8192], P('row', 'tensor'), may hold values from -0.0625 to 0.0625
- embed_weight: bfloat16 [8192, 8192], P('row', 'tensor'), may hold values from -0.0625 to 0.0625
Outputs:
- draft_hidden: bfloat16 [128, 8, 8192], P('row', None, 'tensor')
- new_state: bfloat16 [128, 128, 64, 256], P('row', 'tensor')
All inputs are finite; a program needn't handle non-finite values.
Results may differ from a plain program's by a relative error of at most 0.0049.
Values may be sent and summed in bfloat16 or wider, within the bound.
A program may use at most 64 MiB of HBM per device.

v0:
```python
import jax
import jax.numpy as jnp
from jax import lax
from jax.sharding import PartitionSpec as P

norm_eps = 1e-05


def body(
    ssm_input,
    gate_input,
    write_vectors,
    read_vectors,
    step_logit,
    step_bias,
    decay_rate,
    skip_gain,
    norm_gain,
    ssm_state,
    accepted,
    out_weight,
    token_embeds,
    feat_weight,
    embed_weight,
):
    highest = lax.Precision.HIGHEST
    row_count, draft_len, channels = ssm_input.shape
    head_count = step_logit.shape[-1]
    head_width = channels // head_count
    embeds_all = lax.all_gather(token_embeds, "tensor", axis=0, tiled=True)
    step_size = jax.nn.softplus(step_logit + step_bias[None, None, :])
    log_decay = jnp.cumsum(-step_size * decay_rate[None, None, :], axis=1)
    x_heads = ssm_input.astype(jnp.float32).reshape(row_count, draft_len, head_count, head_width)
    intersection = jnp.einsum(
        "rtn,rsn->rts", read_vectors, write_vectors, preferred_element_type=jnp.float32
    )
    positions = jnp.arange(draft_len)
    lower = (positions[None, :] <= positions[:, None])[None, :, :, None]
    gap = log_decay[:, :, None, :] - log_decay[:, None, :, :]
    kernel_mix = (
        jnp.where(lower, jnp.exp(jnp.where(lower, gap, 0.0)), 0.0)
        * intersection[:, :, :, None]
        * step_size[:, None, :, :]
    )
    intra = jnp.einsum("rtsh,rshp->rthp", kernel_mix, x_heads, precision=highest)
    carried = jnp.einsum(
        "rtn,rhpn->rthp", read_vectors, ssm_state, preferred_element_type=jnp.float32
    )
    mixed = (
        jnp.exp(log_decay)[:, :, :, None] * carried
        + intra
        + skip_gain[None, None, :, None] * x_heads
    )
    gated = mixed.reshape(row_count, draft_len, channels) * jax.nn.silu(
        gate_input.astype(jnp.float32)
    )
    square_total = lax.psum(jnp.sum(gated * gated, axis=-1), "tensor")
    mean_square = square_total / (channels * lax.axis_size("tensor"))
    normed = (
        gated * lax.rsqrt(mean_square[:, :, None] + norm_eps) * norm_gain[None, None, :]
    ).astype(jnp.bfloat16)
    normed_flat = normed.reshape(row_count * draft_len, channels)
    partial_out = jnp.dot(
        lax.all_gather(normed_flat, "row", axis=0, tiled=True),
        out_weight,
        preferred_element_type=jnp.float32,
    )
    feature = lax.psum(partial_out, "tensor").astype(jnp.bfloat16)
    embeds_flat = embeds_all.reshape(feature.shape[0], embeds_all.shape[-1])
    summed_rows = lax.psum_scatter(
        jnp.dot(feature, feat_weight, preferred_element_type=jnp.float32)
        + jnp.dot(embeds_flat, embed_weight, preferred_element_type=jnp.float32),
        "row",
        scatter_dimension=0,
        tiled=True,
    )
    used = (positions[None, :] <= accepted[:, None]).astype(jnp.float32)
    draft_hidden = (summed_rows.reshape(row_count, draft_len, -1) * used[:, :, None]).astype(
        jnp.bfloat16
    )
    padded_log = jnp.concatenate(
        [jnp.zeros((row_count, 1, head_count), jnp.float32), log_decay], axis=1
    )
    chosen = (jnp.arange(draft_len + 1)[None, :] == accepted[:, None]).astype(jnp.float32)
    end_log = jnp.einsum("rk,rkh->rh", chosen, padded_log, precision=highest)
    kept = (positions[None, :] < accepted[:, None])[:, :, None]
    weight_in = (
        jnp.where(kept, jnp.exp(jnp.where(kept, end_log[:, None, :] - log_decay, 0.0)), 0.0)
        * step_size
    )
    weighted_x = weight_in[:, :, :, None] * x_heads
    added = jnp.einsum(
        "rshp,rsn->rhpn", weighted_x, write_vectors.astype(jnp.float32), precision=highest
    )
    new_state = (jnp.exp(end_log)[:, :, None, None] * ssm_state.astype(jnp.float32) + added).astype(
        jnp.bfloat16
    )
    return (draft_hidden, new_state)


def solution(mesh):
    in_specs = (
        P("row", None, "tensor"),
        P("row", None, "tensor"),
        P("row", None, "tensor"),
        P("row", None, "tensor"),
        P("row", None, "tensor"),
        P("tensor"),
        P("tensor"),
        P("tensor"),
        P("tensor"),
        P("row", "tensor", None, None),
        P("row"),
        P("tensor", "row"),
        P("tensor", None, "row"),
        P("row", "tensor"),
        P("row", "tensor"),
    )
    out_specs = (P("row", None, "tensor"), P("row", "tensor", None, None))
    return jax.shard_map(body, mesh=mesh, in_specs=in_specs, out_specs=out_specs, check_vma=False)
```

profile of v0, /device:TPU:6, one launch (start us, length us, event | category | flops | bytes accessed | tf_op | source)
XLA Modules:
  0.0 285.9 jit_solution(7767640421601534058)
XLA Ops:
  7.3 0.8 fusion.32
  8.1 0.7 iota_compare_fusion.1
  8.8 0.7 negate_multiply_fusion
  9.6 0.1 copy.31
  9.7 0.1 fusion.26
  9.9 0.1 select_multiply_fusion
  10.0 0.9 reshape.93
  10.9 0.9 fusion.35
  11.8 1.7 convolution_multiply_fusion
  13.5 1.0 fusion.1
  14.5 0.1 reshape.95
  14.6 0.1 multiply_reduce_fusion
  14.7 36.5 %psum.14 = f32[4,8]{1,0:T(4,128)S(1)} all-reduce(f32[4,8]{1,0:T(4,128)S(1)} %multiply_reduce_fusion), channel_id=1, replica_groups=mesh['row'=32,'tensor'=16] {'tensor'}, use_global_device_ids=true, to_apply=%region_2.3 | all-reduce | flops 32 | bytes 256 | tf_op jit(solution)/shard_map/psum | solution.py:57
  51.2 0.7 fusion.25
  52.0 29.0 %all_gather.7 = bf16[128,8,256]{2,1,0:T(8,128)(2,1)S(1)} all-gather(bf16[8,8,256]{2,1,0:T(8,128)(2,1)S(1)} %copy-done.6), channel_id=1, replica_groups=mesh['row'=32,'tensor'=16] {'tensor'}, dimensions={0}, use_global_device_ids=true | all-gather | bytes 557056 | tf_op jit(solution)/shard_map/all_gather | solution.py:30
  81.0 24.8 %all-gather.2.cloned.1.call-done = bf16[1024,512]{1,0:T(8,128)(2,1)} async-done(((bf16[32,512]{1,0:T(8,128)(2,1)}), bf16[1024,512]{1,0:T(8,128)(2,1)}) %all-gather.2.cloned.1.call-update) | async-done | bytes 1048592 | tf_op jit(solution)/shard_map/all_gather | solution.py:64
  105.8 1.7 fusion.36
  107.5 70.1 %all-reduce.2 = bf16[1024,256]{1,0:T(8,128)(2,1)S(1)} all-reduce(f32[1024,256]{1,0:T(8,128)S(1)} %fusion.36), channel_id=1, replica_groups=mesh['row'=32,'tensor'=16] {'tensor'}, use_global_device_ids=true, to_apply=%region_3.4 | all-reduce | flops 262144 | bytes 1572864 | tf_op jit(solution)/shard_map/psum | solution.py:68
  177.6 0.4 fusion.37
  178.1 1.8 convolution_add_fusion
  180.0 1.1 copy-done.1
  181.1 2.4 add_convert_fusion
  183.5 94.1 %reduce-scatter.2.cloned.1.call-done = f32[32,512]{1,0:T(8,128)} async-done(((f32[1024,512]{1,0:T(8,128)}), f32[32,512]{1,0:T(8,128)}) %reduce-scatter.2.cloned.1.call-update) | async-done | bytes 65552 | tf_op jit(solution)/shard_map/reduce_scatter | solution.py:70
  277.6 1.5 fusion.15
  (27 shorter events, 0.4 us)
Async XLA Ops:
  7.2 170.5 %copy-start = (bf16[256,512]{1,0:T(8,128)(2,1)S(1)}, bf16[256,512]{1,0:T(8,128)(2,1)}, u32[]{:S(2)}) copy-start(bf16[256,512]{1,0:T(8,128)(2,1)} %param.28) | copy-start | bytes 786436
  7.2 7.4 %copy-start.4 = (bf16[4,8,512]{2,1,0:T(8,128)(2,1)S(1)}, bf16[4,8,512]{2,1,0:T(8,128)(2,1)}, u32[]{:S(2)}) copy-start(bf16[4,8,512]{2,1,0:T(8,128)(2,1)} %param.16) | copy-start | bytes 98308
  7.2 44.1 %copy-start.7 = (f32[512]{0:T(512)S(1)}, f32[512]{0:T(512)}, u32[]{:S(2)}) copy-start(f32[512]{0:T(512)} %param.23) | copy-start | bytes 6148
  7.2 44.8 %copy-start.6 = (bf16[8,8,256]{2,1,0:T(8,128)(2,1)S(1)}, bf16[8,8,256]{2,1,0:T(8,128)(2,1)}, u32[]{:S(2)}) copy-start(bf16[8,8,256]{2,1,0:T(8,128)(2,1)} %param.27) | copy-start | bytes 98308
  7.2 98.6 %copy-start.2 = (bf16[512,256]{1,0:T(8,128)(2,1)S(1)}, bf16[512,256]{1,0:T(8,128)(2,1)}, u32[]{:S(2)}) copy-start(bf16[512,256]{1,0:T(8,128)(2,1)} %param.26) | copy-start | bytes 786436
  7.2 98.6 %all-gather.2.cloned.1.call-start = ((), (), s32[]{:S(2)}) async-start(), calls=%async_computation.1 | async-start | bytes 1081344 | tf_op jit(solution)/shard_map/all_gather | solution.py:64
  52.0 225.6 %reduce-scatter.2.cloned.1.call-start = ((), (), s32[]{:S(2)}) async-start(), calls=%async_computation.2 | async-start | bytes 2162688 | tf_op jit(solution)/shard_map/reduce_scatter | solution.py:70
  107.5 70.6 %copy-start.3 = (bf16[256,512]{1,0:T(8,128)(2,1)S(1)}, bf16[256,512]{1,0:T(8,128)(2,1)}, u32[]{:S(2)}) copy-start(bf16[256,512]{1,0:T(8,128)(2,1)} %param.29) | copy-start | bytes 786436
  179.8 1.2 copy-start.1
  179.8 1.2 copy-start.5
Sparse Core Ops, SparseCore 0:
  52.1 53.6 all-gather.1
  180.0 97.5 reduce-scatter.1
where the time goes:
time: 287 us; the launch traced here: 286 us
  blocking collectives  136 us (47%)
  waiting for transfers between devices  119 us (41%)
  between operations  14.2 us (5%)
  matrix products  10 us (3%)
  other arithmetic  4.73 us (2%)
    reduce_scatter x1, waiting for transfers between devices, body(): lax.psum_scatter(jnp.dot(feature, feat_weight, preferred_element_type=jnp...  94.1 us
    psum x1, blocking collectives, body(): feature = lax.psum(partial_out, 'tensor').astype(jnp.bfloat16)  70.1 us
    psum x1, blocking collectives, body(): square_total = lax.psum(jnp.sum(gated * gated, axis=-1), 'tensor')  36.5 us
    all_gather x1, blocking collectives, body(): embeds_all = lax.all_gather(token_embeds, 'tensor', axis=0, tiled=True)  29 us
    all_gather x1, waiting for transfers between devices, body(): lax.all_gather(normed_flat, 'row', axis=0, tiled=True)  24.8 us
  transfers between devices with their start and end apart: 2, of which 2 were waited for; matrix products, arithmetic and copies ran while one was open for 1% of the time, Pallas kernels for 0%

commit v1 on v0

v1 whole, which is shorter than its diff:
```python
import functools

import jax
import jax.numpy as jnp
from jax import lax
from jax.experimental import pallas as pl
from jax.experimental.pallas import tpu as pltpu
from jax.sharding import PartitionSpec as P

norm_eps = 1e-05
MESH = pl.DeviceIdType.MESH
f32 = jnp.float32
bf16 = jnp.bfloat16


def nt_dot(a, b):
    return lax.dot_general(a, b, (((1,), (1,)), ((), ())), preferred_element_type=f32)


def split3(v):
    hi = v.astype(bf16).astype(f32)
    mid = (v - hi).astype(bf16).astype(f32)
    return hi, mid, v - hi - mid


def kernel(
    x_ref, gate_ref, b_ref, c_ref, logit_ref, bias_ref, decay_ref, skip_ref, gain_ref, acc_ref, emb_ref,
    state_hbm, wo_hbm, wf_hbm, we_hbm,
    draft_ref, ns_hbm,
    state_v, ns_v, wo, wf, we, em_own, em, g_buf, snd, r1, s_sum, s_snd, r2, feat, q_buf, d_snd, d_rcv,
    ssq_own, ssq_rcv, sc_buf,
    loc_sem, sib_s, sib_r, ez_s, ez_r, ag_s, ag_r, sq_s, sq_r, sc_s, sc_r, rs_s, rs_r, fg_s, fg_r, xr_s, xr_r,
):
    row = lax.axis_index("row")
    z = lax.axis_index("tensor")
    core = lax.rem(row, 2)
    chip = row // 2
    cx = chip // 4
    cy = lax.rem(chip, 4)
    zl = lax.rem(z, 4)
    zh = z // 4
    sib = (row + 1 - 2 * core, z)

    def zp(d):
        return (row, lax.rem(z + (d + 16), 16))

    def xyp(dx, dy):
        return ((lax.rem(cx + (dx + 4), 4) * 4 + lax.rem(cy + (dy + 4), 4)) * 2 + core, z)

    xy_all = [(a, b) for a in range(4) for b in range(4) if (a, b) != (0, 0)]
    barrier = pltpu.get_barrier_semaphore()
    peers = [sib] + [zp(d) for d in range(1, 16)] + [xyp(a, b) for a, b in xy_all]
    for p in peers:
        pl.semaphore_signal(barrier, inc=1, device_id=p, device_id_type=MESH)

    def rc(src, dst, ss, rs, dev):
        c = pltpu.make_async_remote_copy(
            src_ref=src, dst_ref=dst, send_sem=ss, recv_sem=rs, device_id=dev, device_id_type=MESH
        )
        c.start()
        return c

    loc = []
    for i, (s, d) in enumerate(
        ((state_hbm, state_v), (wo_hbm, wo.at[0]), (we_hbm, we.at[0]), (wf_hbm, wf.at[0]))
    ):
        c = pltpu.make_async_copy(s, d, loc_sem.at[i])
        c.start()
        loc.append(c)

    em_own[...] = emb_ref[...].astype(f32).reshape(2, 32, 256).astype(bf16)
    em[zl, zh, 0] = em_own[core]

    pl.semaphore_wait(barrier, len(peers))
    pend = []
    c_em = rc(em_own.at[1 - core], em.at[zl, zh, 1], sib_s.at[0], sib_r.at[0], sib)
    c_wo = rc(wo_hbm, wo.at[1], sib_s.at[1], sib_r.at[1], sib)
    c_we = rc(we_hbm, we.at[1], sib_s.at[2], sib_r.at[2], sib)
    c_wf = rc(wf_hbm, wf.at[1], sib_s.at[3], sib_r.at[3], sib)
    pend += [c_em, c_wo, c_we, c_wf]

    c_em.wait_recv()
    em_far = [
        rc(em.at[zl, zh], em.at[zl, zh], ez_s.at[m], ez_r.at[m], zp(4 * m)) for m in (2, 1, 3)
    ]
    pend += em_far

    x3 = x_ref[...].astype(f32)
    c3 = c_ref[...].astype(f32)
    b3 = b_ref[...].astype(f32)
    lane_head = lax.broadcasted_iota(jnp.int32, (8, 512), 1) // 64
    pick = (lane_head == lax.broadcasted_iota(jnp.int32, (8, 512), 0)).astype(f32)

    def expand(v):
        return jnp.dot(v, pick, precision=lax.Precision.HIGHEST, preferred_element_type=f32)

    step = jax.nn.softplus(logit_ref[...].reshape(32, 8) + bias_ref[...])
    step_x = expand(step)
    decay_x = expand(jnp.broadcast_to(decay_ref[...], (8, 8)))[0:1]
    skip_x = expand(jnp.broadcast_to(skip_ref[...], (8, 8)))[0:1]
    log_x = -step_x * decay_x
    t_in = lax.rem(lax.broadcasted_iota(jnp.int32, (32, 512), 0), 8)
    for k in (1, 2, 4):
        log_x = log_x + jnp.where(t_in >= k, pltpu.roll(log_x, k, 0), 0.0)
    log3 = log_x.reshape(4, 8, 512)
    step3 = step_x.reshape(4, 8, 512)
    sx3 = step3 * x3
    t3 = lax.broadcasted_iota(jnp.int32, (4, 8, 512), 1)
    gmat = [nt_dot(c3[r].astype(bf16), b3[r].astype(bf16)) for r in range(4)]
    intra = skip_x * x3
    for s in range(8):
        keep = t3 >= s
        e = jnp.where(keep, jnp.exp(jnp.where(keep, log3 - log3[:, s : s + 1, :], 0.0)), 0.0)
        gcol = jnp.stack([gmat[r][:, s : s + 1] for r in range(4)], axis=0)
        intra = intra + e * gcol * sx3[:, s : s + 1, :]
    loc[0].wait()
    carried = jnp.stack([nt_dot(c3[r].astype(bf16), state_v[r]) for r in range(4)], axis=0)
    mixed = jnp.exp(log3) * carried + intra
    gate = gate_ref[...].astype(f32)
    gated = (mixed * (gate / (1.0 + jnp.exp(-gate)))).reshape(32, 512)
    g_buf[0, 0] = (gated * gain_ref[...]).astype(bf16)
    ag = {}
    for a, b in xy_all:
        i = a * 4 + b
        ag[i] = rc(g_buf.at[0, 0], g_buf.at[a, b], ag_s.at[i], ag_r.at[i], xyp(a, b))
    ssq = jnp.sum(gated * gated, axis=1, keepdims=True)
    eye = lax.broadcasted_iota(jnp.int32, (32, 128), 0) == lax.broadcasted_iota(jnp.int32, (32, 128), 1)
    ssq_own[...] = jnp.sum(jnp.where(eye, ssq, 0.0), axis=0, keepdims=True)
    sq = [rc(ssq_own, ssq_rcv.at[d], sq_s.at[d], sq_r.at[d], zp(d)) for d in range(1, 16)]

    for r in range(4):
        k = acc_ref[r]
        t2 = t3[r]
        end = jnp.sum(jnp.where(t2 == k - 1, log3[r], 0.0), axis=0, keepdims=True)
        kept = t2 < k
        w = jnp.where(kept, jnp.exp(jnp.where(kept, end - log3[r], 0.0)), 0.0) * sx3[r]
        hi, mid, lo = split3(w)
        turned = jnp.transpose(
            jnp.concatenate([hi, mid, lo, jnp.broadcast_to(jnp.exp(end), (8, 512))], axis=0)
        )
        b24 = jnp.concatenate([b3[r], b3[r], b3[r]], axis=0).astype(bf16)
        add = jnp.dot(turned[:, 0:24].astype(bf16), b24, preferred_element_type=f32)
        ns_v[r] = (turned[:, 24:25] * state_v[r].astype(f32) + add).astype(bf16)
    ns_out = pltpu.make_async_copy(ns_v, ns_hbm, loc_sem.at[4])
    ns_out.start()

    for c in em_far:
        c.wait_recv()
    em_near = [
        rc(em.at[zl], em.at[zl], ez_s.at[4], ez_r.at[4], zp(1)),
        rc(em.at[zl], em.at[zl], ez_s.at[5], ez_r.at[5], zp(-1)),
        rc(em.at[zl, pl.ds(0, 2)], em.at[zl, pl.ds(0, 2)], ez_s.at[6], ez_r.at[6], zp(2)),
        rc(em.at[zl, pl.ds(2, 2)], em.at[zl, pl.ds(2, 2)], ez_s.at[7], ez_r.at[7], zp(-2)),
    ]
    pend += em_near

    for c in ag.values():
        c.wait_recv()
    loc[1].wait()
    c_wo.wait_recv()
    near = []
    for j, d in enumerate((2, 1, -1, 0)):
        g = g_buf[lax.rem(z + (d + 4), 4)].reshape(128, 512)
        for h in range(2):
            part = jnp.dot(g, wo[h], preferred_element_type=f32).reshape(4, 32, 256)
            cols = pl.ds(256 * h, 256)
            if d == 0:
                s_sum[:, :, cols] = part
            else:
                snd[j, :, :, cols] = part.astype(bf16)
        if d == 2:
            for h, dd in ((0, 2), (1, -2)):
                cols = pl.ds(256 * h, 256)
                near.append(
                    rc(snd.at[0, :, :, cols], r1.at[0, :, :, cols], rs_s.at[h], rs_r.at[h], zp(dd))
                )
        elif d != 0:
            near.append(rc(snd.at[j], r1.at[j], rs_s.at[1 + j], rs_r.at[1 + j], zp(d)))
    pend += near

    total = ssq_own[...]
    for c in sq:
        c.wait_recv()
    for d in range(1, 16):
        total = total + ssq_rcv[d]
    sc_buf[0] = lax.rsqrt(total / 8192.0 + norm_eps)
    sc = [
        rc(sc_buf.at[0], sc_buf.at[a * 4 + b], sc_s.at[a * 4 + b], sc_r.at[a * 4 + b], xyp(a, b))
        for a, b in xy_all
    ]
    pend += sq + sc + list(ag.values())

    for c in near:
        c.wait_recv()
    s_sum[...] = s_sum[...] + r1[0].astype(f32) + r1[1].astype(f32) + r1[2].astype(f32)
    s_snd[...] = s_sum[...].astype(bf16)
    far = []
    for m in (2, 1, 3):
        far.append(
            rc(s_snd.at[lax.rem(zh + m, 4)], r2.at[m], rs_s.at[4 + m], rs_r.at[4 + m], zp(4 * m))
        )
    pend += far

    loc[2].wait()
    c_we.wait_recv()
    for c in em_near:
        c.wait_recv()
    for a in range(4):
        ex = lax.rem(cx + (4 - a), 4)
        es = [em[lax.rem(cy + (4 - b), 4), ex] for b in range(4)]
        q = 0.0
        for h in range(2):
            e = jnp.concatenate([v[h] for v in es], axis=0)
            q = q + jnp.dot(e, we[h], preferred_element_type=f32)
        q_buf[a] = q.reshape(4, 32, 512)

    for c in far:
        c.wait_recv()
    feat[zl, zh] = (
        s_sum[zh] + r2[1].astype(f32) + r2[2].astype(f32) + r2[3].astype(f32)
    ).astype(bf16)
    f_far = [
        rc(feat.at[zl, zh], feat.at[zl, zh], fg_s.at[m], fg_r.at[m], zp(4 * m)) for m in (2, 1, 3)
    ]
    loc[3].wait()
    c_wf.wait_recv()
    for c in sc:
        c.wait_recv()
    for c in f_far:
        c.wait_recv()
    f_near = [
        rc(feat.at[zl, pl.ds(0, 2)], feat.at[zl, pl.ds(0, 2)], fg_s.at[6], fg_r.at[6], zp(2)),
        rc(feat.at[zl, pl.ds(2, 2)], feat.at[zl, pl.ds(2, 2)], fg_s.at[7], fg_r.at[7], zp(-2)),
        rc(feat.at[zl], feat.at[zl], fg_s.at[4], fg_r.at[4], zp(1)),
        rc(feat.at[zl], feat.at[zl], fg_s.at[5], fg_r.at[5], zp(-1)),
    ]
    pend += f_far + f_near
    for c in f_near:
        c.wait_recv()

    xr = []
    mine = None
    for a in (3, 2, 1, 0):
        f = feat[a].reshape(128, 512)
        y = jnp.dot(f[:, 0:256], wf[0], preferred_element_type=f32)
        y = y + jnp.dot(f[:, 256:512], wf[1], preferred_element_type=f32)
        for b in range(4):
            i = a * 4 + b
            scale = jnp.sum(jnp.where(eye, sc_buf[i], 0.0), axis=1, keepdims=True)
            out = y[32 * b : 32 * b + 32] * scale + q_buf[a, b]
            if i == 0:
                mine = out
            else:
                d_snd[a, b] = out.astype(bf16)
                xr.append(rc(d_snd.at[a, b], d_rcv.at[a, b], xr_s.at[i], xr_r.at[i], xyp(-a, -b)))
    for c in xr:
        c.wait_recv()
    for a, b in xy_all:
        mine = mine + d_rcv[a, b].astype(f32)
    mine = mine.reshape(4, 8, 512)
    for r in range(4):
        draft_ref[r] = jnp.where(t3[r] <= acc_ref[r], mine[r], 0.0).astype(bf16)
    ns_out.wait()
    for c in pend + xr:
        c.wait_send()


def body(
    ssm_input, gate_input, write_vectors, read_vectors, step_logit, step_bias, decay_rate, skip_gain,
    norm_gain, ssm_state, accepted, out_weight, token_embeds, feat_weight, embed_weight,
):
    vm = pl.BlockSpec(memory_space=pltpu.VMEM)
    hbm = pl.BlockSpec(memory_space=pl.ANY)
    dma = pltpu.SemaphoreType.DMA
    draft, new_state = pl.pallas_call(
        kernel,
        out_shape=(
            jax.ShapeDtypeStruct((4, 8, 512), bf16),
            jax.ShapeDtypeStruct((4, 512, 256), bf16),
        ),
        in_specs=[vm] * 9 + [pl.BlockSpec(memory_space=pltpu.SMEM), vm] + [hbm] * 4,
        out_specs=(vm, hbm),
        scratch_shapes=[
            pltpu.VMEM((4, 512, 256), bf16),
            pltpu.VMEM((4, 512, 256), bf16),
            pltpu.VMEM((2, 512, 256), bf16),
            pltpu.VMEM((2, 256, 512), bf16),
            pltpu.VMEM((2, 256, 512), bf16),
            pltpu.VMEM((2, 32, 256), bf16),
            pltpu.VMEM((4, 4, 2, 32, 256), bf16),
            pltpu.VMEM((4, 4, 32, 512), bf16),
            pltpu.VMEM((3, 4, 32, 512), bf16),
            pltpu.VMEM((3, 4, 32, 512), bf16),
            pltpu.VMEM((4, 32, 512), f32),
            pltpu.VMEM((4, 32, 512), bf16),
            pltpu.VMEM((4, 32, 512), bf16),
            pltpu.VMEM((4, 4, 32, 512), bf16),
            pltpu.VMEM((4, 4, 32, 512), f32),
            pltpu.VMEM((4, 4, 32, 512), bf16),
            pltpu.VMEM((4, 4, 32, 512), bf16),
            pltpu.VMEM((1, 128), f32),
            pltpu.VMEM((16, 1, 128), f32),
            pltpu.VMEM((16, 1, 128), f32),
            dma((5,)),
            dma((4,)), dma((4,)),
            dma((8,)), dma((8,)),
            dma((16,)), dma((16,)),
            dma((16,)), dma((16,)),
            dma((16,)), dma((16,)),
            dma((8,)), dma((8,)),
            dma((8,)), dma((8,)),
            dma((16,)), dma((16,)),
        ],
        compiler_params=pltpu.CompilerParams(
            collective_id=0, has_side_effects=True, vmem_limit_bytes=40 * 1024 * 1024
        ),
        name="verify_step",
    )(
        ssm_input, gate_input, write_vectors, read_vectors, step_logit,
        step_bias.reshape(1, 8), decay_rate.reshape(1, 8), skip_gain.reshape(1, 8),
        norm_gain.reshape(1, 512), accepted, token_embeds,
        ssm_state.reshape(4, 512, 256), out_weight, feat_weight, embed_weight,
    )
    return draft, new_state.reshape(4, 8, 64, 256)


def solution(mesh):
    in_specs = (
        P("row", None, "tensor"),
        P("row", None, "tensor"),
        P("row", None, "tensor"),
        P("row", None, "tensor"),
        P("row", None, "tensor"),
        P("tensor"),
        P("tensor"),
        P("tensor"),
        P("tensor"),
        P("row", "tensor", None, None),
        P("row"),
        P("tensor", "row"),
        P("tensor", None, "row"),
        P("row", "tensor"),
        P("row", "tensor"),
    )
    out_specs = (P("row", None, "tensor"), P("row", "tensor", None, None))
    return jax.shard_map(body, mesh=mesh, in_specs=in_specs, out_specs=out_specs, check_vma=False)
```

time: 287 us -> 87.5 us (0.30)
  the two profiles are of different devices: /device:TPU:6 before, /device:TPU:36 now
where the time goes in v1:
time: 87.5 us; the launch traced here: 86.9 us
  Pallas kernels  75.4 us (86%)
  local copies, waits for them, and re-layouts  10.8 us (12%)
    pallas_call x1, Pallas kernels, body(): pl.pallas_call(kernel, out_shape=(jax.ShapeDtypeStruct((4, 8, 512), bf16)...  75.4 us
    unnamed x32, local copies, waits for them, and re-layouts  10.8 us

profile of v1, /device:TPU:36, one launch (start us, length us, event | category | flops | bytes accessed | tf_op | source)
XLA Modules:
  0.0 86.9 jit_solution(2512815898514196763)
XLA Ops:
  0.6 0.0 copy-start.14
  0.6 0.0 copy-start.10
  0.7 0.0 copy-start.11
  0.7 0.0 copy-start.12
  0.7 0.0 copy-start.13
  0.7 0.6 copy-done.14
  1.3 0.0 copy-done.10
  1.3 0.0 copy-done.11
  1.3 0.0 copy-done.12
  1.3 0.0 copy-done.13
  1.4 0.0 copy-start
  1.4 1.2 %copy-done = bf16[4,8,64,256]{3,2,1,0:T(8,128)(2,1)S(1)} copy-done((bf16[4,8,64,256]{3,2,1,0:T(8,128)(2,1)S(1)}, bf16[4,8,64,256]{3,2,1,0:T(8,128)(2,1)}, u32[]{:S(2)}) %copy-start) | copy-done | bytes 1048600
  2.6 0.9 %copy-done.1 = bf16[512,256]{1,0:T(8,128)(2,1)S(1)} copy-done((bf16[512,256]{1,0:T(8,128)(2,1)S(1)}, bf16[512,256]{1,0:T(8,128)(2,1)}, u32[]{:S(2)}) %copy-start.1) | copy-done | bytes 262168
  3.5 0.9 %copy-done.2 = bf16[256,512]{1,0:T(8,128)(2,1)S(1)} copy-done((bf16[256,512]{1,0:T(8,128)(2,1)S(1)}, bf16[256,512]{1,0:T(8,128)(2,1)}, u32[]{:S(2)}) %copy-start.2) | copy-done | bytes 262168
  4.5 0.9 %copy-done.3 = bf16[256,512]{1,0:T(8,128)(2,1)S(1)} copy-done((bf16[256,512]{1,0:T(8,128)(2,1)S(1)}, bf16[256,512]{1,0:T(8,128)(2,1)}, u32[]{:S(2)}) %copy-start.3) | copy-done | bytes 262168
  5.4 0.8 copy-done.4
  6.2 0.8 copy-done.5
  7.0 0.8 copy-done.6
  7.7 0.7 copy-done.7
  8.4 0.7 copy-done.8
  9.1 0.7 copy-done.9
  9.9 75.4 %verify_step.1 = (bf16[4,8,512]{2,1,0:T(8,128)(2,1)S(1)}, bf16[4,512,256]{2,1,0:T(8,128)(2,1)S(1)}) custom-call(bf16[4,8,512]{2,1,0:T(8,128)(2,1)S(1)} %copy-done.4, bf16[4,8,512]{2,1,0:T(8,128)(2,1)S(1)} %copy-done.5, bf16[4,8,256]{2,1,0:T(8,128)(2,1)S(1)} %copy-done.7, bf16[4,8,256]{2,1,0:T(8,128)(2,1)S(1)} %copy-done.8, f32[4,8,8]{2,1,0:T(8,128)S(1)} %copy-done.9, ...), custom_call_target="tpu_custom_call" | custom-call | tf_op jit(solution)/shard_map/verify_step/pallas_call | solution.py:275
  85.3 0.6 copy.19
  85.9 1.0 %copy.20 = bf16[4,8,64,256]{3,2,1,0:T(8,128)(2,1)} copy(bf16[4,8,64,256]{3,2,1,0:T(8,128)(2,1)S(1)} %bitcast.6) | data formatting | bytes 2097152
  (9 shorter events, 0.0 us)
Async XLA Ops:
  0.6 0.7 copy-start.14
  0.6 0.7 copy-start.10
  0.7 0.7 copy-start.11
  0.7 0.7 copy-start.12
  0.7 0.7 copy-start.13
  1.4 1.2 %copy-start = (bf16[4,8,64,256]{3,2,1,0:T(8,128)(2,1)S(1)}, bf16[4,8,64,256]{3,2,1,0:T(8,128)(2,1)}, u32[]{:S(2)}) copy-start(bf16[4,8,64,256]{3,2,1,0:T(8,128)(2,1)} %param.24) | copy-start | bytes 3145732
  2.6 0.9 %copy-start.1 = (bf16[512,256]{1,0:T(8,128)(2,1)S(1)}, bf16[512,256]{1,0:T(8,128)(2,1)}, u32[]{:S(2)}) copy-start(bf16[512,256]{1,0:T(8,128)(2,1)} %wo_hbm.1) | copy-start | bytes 786436
  3.5 0.9 %copy-start.2 = (bf16[256,512]{1,0:T(8,128)(2,1)S(1)}, bf16[256,512]{1,0:T(8,128)(2,1)}, u32[]{:S(2)}) copy-start(bf16[256,512]{1,0:T(8,128)(2,1)} %wf_hbm.1) | copy-start | bytes 786436
  4.5 0.9 %copy-start.3 = (bf16[256,512]{1,0:T(8,128)(2,1)S(1)}, bf16[256,512]{1,0:T(8,128)(2,1)}, u32[]{:S(2)}) copy-start(bf16[256,512]{1,0:T(8,128)(2,1)} %we_hbm.1) | copy-start | bytes 786436
  5.4 0.8 copy-start.4
  6.2 0.8 copy-start.5
  6.9 0.8 copy-start.6
  7.7 0.7 copy-start.7
  8.4 0.7 copy-start.8
  9.1 0.7 copy-start.9

commit v2 on v1

v2 whole, which is shorter than its diff:
```python
import functools

import jax
import jax.numpy as jnp
from jax import lax
from jax.experimental import pallas as pl
from jax.experimental.pallas import tpu as pltpu
from jax.sharding import PartitionSpec as P

norm_eps = 1e-05
MESH = pl.DeviceIdType.MESH
f32 = jnp.float32
bf16 = jnp.bfloat16


def nt_dot(a, b):
    return lax.dot_general(a, b, (((1,), (1,)), ((), ())), preferred_element_type=f32)


def split3(v):
    hi = v.astype(bf16).astype(f32)
    mid = (v - hi).astype(bf16).astype(f32)
    return hi, mid, v - hi - mid


def kernel(
    x_hbm, gate_hbm, b_hbm, c_hbm, logit_hbm, bias_hbm, decay_hbm, skip_hbm, gain_hbm, state_hbm, acc_hbm,
    wo_hbm, emb_hbm, wf_hbm, we_hbm,
    draft_hbm, ns_hbm,
    x_ref, gate_ref, b_ref, c_ref, logit_ref, bias_ref, decay_ref, skip_ref, gain_ref, acc_ref, emb_ref,
    draft_ref, ns_ref, state_v, wo, wf, we, em_own, em, g_buf, p_own, p_snd, r1, s_snd, r2, feat, q_buf, d_snd, d_rcv,
    ssq_own, ssq_rcv, sc_buf,
    loc_sem, sib_s, sib_r, ez_s, ez_r, en_s, en_r, ag_s, ag_r, sq_s, sq_r, sc_s, sc_r, rs_s, rs_r,
    rf_s, rf_r, ff_s, ff_r, fn_s, fn_r, xr_s, xr_r,
):
    groups = (6, -6, 3, -3, 0)
    slot = {g: i for i, g in enumerate(groups)}
    row = lax.axis_index("row")
    z = lax.axis_index("tensor")
    core = lax.rem(row, 2)
    chip = row // 2
    cx = chip // 4
    cy = lax.rem(chip, 4)
    sib = (row + 1 - 2 * core, z)

    def at(d):
        return lax.rem(z + (d + 16), 16)

    def zp(d):
        return (row, at(d))

    def xyp(dx, dy):
        return ((lax.rem(cx + (dx + 4), 4) * 4 + lax.rem(cy + (dy + 4), 4)) * 2 + core, z)

    xy_all = [(a, b) for a in range(4) for b in range(4) if (a, b) != (0, 0)]
    barrier = pltpu.get_barrier_semaphore()
    peers = [sib] + [(sib[0], at(d)) for d in (6, -6, 3, -3)] + [zp(d) for d in range(1, 16)] + [xyp(a, b) for a, b in xy_all]
    for p in peers:
        pl.semaphore_signal(barrier, inc=1, device_id=p, device_id_type=MESH)

    def rc(src, dst, ss, rs, dev):
        c = pltpu.make_async_remote_copy(
            src_ref=src, dst_ref=dst, send_sem=ss, recv_sem=rs, device_id=dev, device_id_type=MESH
        )
        c.start()
        return c

    def wait_arrival(ref, sem):
        pltpu.make_async_remote_copy(
            src_ref=ref, dst_ref=ref, send_sem=sem, recv_sem=sem, device_id=sib, device_id_type=MESH
        ).wait_recv()

    def wait_leave(ref, sem):
        pltpu.make_async_remote_copy(
            src_ref=ref, dst_ref=ref, send_sem=sem, recv_sem=sem, device_id=sib, device_id_type=MESH
        ).wait_send()

    loc = []
    for i, (s, d) in enumerate(
        (
            (emb_hbm, emb_ref), (logit_hbm, logit_ref), (bias_hbm, bias_ref), (decay_hbm, decay_ref),
            (skip_hbm, skip_ref), (acc_hbm, acc_ref), (x_hbm, x_ref), (c_hbm, c_ref), (b_hbm, b_ref),
            (gate_hbm, gate_ref), (gain_hbm, gain_ref), (state_hbm, state_v), (wo_hbm, wo.at[0]),
            (we_hbm, we.at[0]), (wf_hbm, wf.at[0]),
        )
    ):
        c = pltpu.make_async_copy(s, d, loc_sem.at[i])
        c.start()
        loc.append(c)
    loc_wo, loc_we, loc_wf = loc[12:]

    loc[0].wait()
    em_own[...] = emb_ref[...].astype(f32).reshape(2, 32, 256).astype(bf16)
    em[z, 0] = em_own[core]

    for c in loc[1:11]:
        c.wait()
    x3 = x_ref[...].astype(f32)
    c3 = c_ref[...].astype(f32)
    b3 = b_ref[...].astype(f32)
    lane_head = lax.broadcasted_iota(jnp.int32, (8, 512), 1) // 64
    pick = (lane_head == lax.broadcasted_iota(jnp.int32, (8, 512), 0)).astype(f32)
    bias = jnp.zeros((1, 8), f32)
    decay_x = jnp.zeros((1, 512), f32)
    skip_x = jnp.zeros((1, 512), f32)
    for h in range(8):
        bias = jnp.where(lax.broadcasted_iota(jnp.int32, (1, 8), 1) == h, bias_ref[h], bias)
        decay_x = jnp.where(lane_head[0:1] == h, decay_ref[h], decay_x)
        skip_x = jnp.where(lane_head[0:1] == h, skip_ref[h], skip_x)

    def expand(v):
        return jnp.dot(v, pick, precision=lax.Precision.HIGHEST, preferred_element_type=f32)

    step = jax.nn.softplus(logit_ref[...].reshape(32, 8) + bias)
    step_x = expand(step)
    log_x = -step_x * decay_x
    t_in = lax.rem(lax.broadcasted_iota(jnp.int32, (32, 512), 0), 8)
    for k in (1, 2, 4):
        log_x = log_x + jnp.where(t_in >= k, pltpu.roll(log_x, k, 0), 0.0)
    log3 = log_x.reshape(4, 8, 512)
    step3 = step_x.reshape(4, 8, 512)
    sx3 = step3 * x3
    t3 = lax.broadcasted_iota(jnp.int32, (4, 8, 512), 1)
    gmat = [nt_dot(c3[r].astype(bf16), b3[r].astype(bf16)) for r in range(4)]
    intra = skip_x * x3
    for s in range(8):
        keep = t3 >= s
        e = jnp.where(keep, jnp.exp(jnp.where(keep, log3 - log3[:, s : s + 1, :], 0.0)), 0.0)
        gcol = jnp.stack([gmat[r][:, s : s + 1] for r in range(4)], axis=0)
        intra = intra + e * gcol * sx3[:, s : s + 1, :]
    loc[11].wait()
    carried = jnp.stack([nt_dot(c3[r].astype(bf16), state_v[r]) for r in range(4)], axis=0)
    mixed = jnp.exp(log3) * carried + intra
    gate = gate_ref[...].astype(f32)
    gated = (mixed * (gate / (1.0 + jnp.exp(-gate)))).reshape(32, 512)
    g_buf[0] = (gated * gain_ref[...].reshape(1, 512)).astype(bf16)
    ssq = jnp.sum(gated * gated, axis=1, keepdims=True)
    eye = lax.broadcasted_iota(jnp.int32, (32, 128), 0) == lax.broadcasted_iota(jnp.int32, (32, 128), 1)
    ssq_own[...] = jnp.sum(jnp.where(eye, ssq, 0.0), axis=0, keepdims=True)

    pl.semaphore_wait(barrier, len(peers))
    def normed_send(o, i):
        rc(g_buf.at[0], g_buf.at[o], ag_s.at[0], ag_r.at[i], xyp(o // 4, lax.rem(o, 4)))

    members = {g: (-1, 0, 1, 2) if g == 6 else (-1, 0, 1) for g in groups}
    for g in groups:
        for d in members[g]:
            o = at(g + d)
            pl.when(o != 0)(functools.partial(normed_send, o, slot[g]))
    c_em = rc(em_own.at[1 - core], em.at[z, 1], sib_s.at[0], sib_r.at[0], sib)
    c_wo = rc(wo_hbm, wo.at[1], sib_s.at[1], sib_r.at[1], sib)
    c_we = rc(we_hbm, we.at[1], sib_s.at[2], sib_r.at[2], sib)
    c_wf = rc(wf_hbm, wf.at[1], sib_s.at[3], sib_r.at[3], sib)

    for g in (6, -6, 3, -3):
        rc(em_own.at[core], em.at[z, 0], ez_s.at[0], ez_r.at[0], zp(g))
        rc(em_own.at[1 - core], em.at[z, 1], ez_s.at[0], ez_r.at[0], (sib[0], at(g)))

    def embeds_near(g):
        o = at(-g)
        if g == 6:
            rc(em.at[o, 0], em.at[o, 0], en_s.at[1], en_r.at[1], zp(2))
        if g == -6:
            rc(em.at[o, 1], em.at[o, 1], en_s.at[2], en_r.at[2], zp(-2))
        rc(em.at[o], em.at[o], en_s.at[0], en_r.at[0], zp(1))
        rc(em.at[o], em.at[o], en_s.at[0], en_r.at[0], zp(-1))

    for d in range(1, 16):
        rc(ssq_own, ssq_rcv.at[d], sq_s.at[0], sq_r.at[0], zp(d))
    c_em.wait_recv()
    embeds_near(0)

    for r in range(4):
        k = acc_ref[r]
        t2 = t3[r]
        end = jnp.sum(jnp.where(t2 == k - 1, log3[r], 0.0), axis=0, keepdims=True)
        kept = t2 < k
        w = jnp.where(kept, jnp.exp(jnp.where(kept, end - log3[r], 0.0)), 0.0) * sx3[r]
        hi, mid, lo = split3(w)
        turned = jnp.transpose(
            jnp.concatenate([hi, mid, lo, jnp.broadcast_to(jnp.exp(end), (8, 512))], axis=0)
        )
        b24 = jnp.concatenate([b3[r], b3[r], b3[r]], axis=0).astype(bf16)
        add = jnp.dot(turned[:, 0:24].astype(bf16), b24, preferred_element_type=f32)
        ns_ref[r] = (turned[:, 24:25] * state_v[r].astype(f32) + add).astype(bf16)
    ns_out = pltpu.make_async_copy(ns_ref, ns_hbm, loc_sem.at[15])
    ns_out.start()

    loc_wo.wait()
    c_wo.wait_recv()
    for g in groups:
        i = slot[g]
        n = len(members[g])
        own_inside = functools.reduce(jnp.logical_or, [at(g + d) == 0 for d in members[g]])
        pl.when(own_inside)(lambda n=n, i=i: wait_arrival(g_buf.at[pl.ds(0, n - 1)], ag_r.at[i]))
        pl.when(jnp.logical_not(own_inside))(lambda n=n, i=i: wait_arrival(g_buf.at[pl.ds(0, n)], ag_r.at[i]))
        rows = jnp.concatenate([g_buf[at(g + d)] for d in members[g]], axis=0)
        for h in range(2):
            part = jnp.dot(rows, wo[h], preferred_element_type=f32).reshape(n, 32, 256)
            cols = pl.ds(256 * h, 256)
            p_own[i, :, cols] = part[1]
            p_snd[i, 0:n, :, cols] = part.astype(bf16)
        rc(p_snd.at[i, 2], r1.at[i, 0], rs_s.at[0], rs_r.at[i], zp(1))
        rc(p_snd.at[i, 0], r1.at[i, 1], rs_s.at[0], rs_r.at[i], zp(-1))
        if g == 6:
            cols = pl.ds(0, 256)
            rc(p_snd.at[0, 3, :, cols], r1.at[i, 2, :, cols], rs_s.at[1], rs_r.at[5], zp(2))
        if g == -6:
            cols = pl.ds(256, 256)
            rc(p_snd.at[0, 3, :, cols], r1.at[i, 2, :, cols], rs_s.at[2], rs_r.at[6], zp(-2))

    for g in groups:
        i = slot[g]
        wait_arrival(r1.at[i, pl.ds(0, 2)], rs_r.at[i])
        p_own[i] = p_own[i] + r1[i, 0].astype(f32) + r1[i, 1].astype(f32)
        if abs(g) == 6:
            cols = pl.ds(0 if g > 0 else 256, 256)
            wait_arrival(r1.at[i, 2, :, cols], rs_r.at[5 if g > 0 else 6])
            p_own[i, :, cols] = p_own[i, :, cols] + r1[i, 2, :, cols].astype(f32)
        if g != 0:
            s_snd[i] = p_own[i].astype(bf16)
            rc(s_snd.at[i], r2.at[i], rf_s.at[0], rf_r.at[0], zp(g))

    wait_arrival(em.at[pl.ds(0, 4)], ez_r.at[0])
    for g in (6, -6, 3, -3):
        embeds_near(g)

    total = ssq_own[...]
    wait_arrival(ssq_rcv.at[pl.ds(1, 15)], sq_r.at[0])
    for d in range(1, 16):
        total = total + ssq_rcv[d]
    sc_buf[0] = lax.rsqrt(total / 8192.0 + norm_eps)
    for a, b in xy_all:
        rc(sc_buf.at[0], sc_buf.at[a * 4 + b], sc_s.at[0], sc_r.at[0], xyp(a, b))

    wait_arrival(r2, rf_r.at[0])
    total = p_own[slot[0]]
    for g in (3, -3, 6, -6):
        total = total + r2[slot[g]].astype(f32)
    feat[z] = total.astype(bf16)
    f_far = {}
    for g in (6, -6, 3, -3):
        f_far[g] = rc(feat.at[z], feat.at[z], ff_s.at[0], ff_r.at[slot[g]], zp(g))

    def forward(g):
        c = feat.at[at(-g)]
        if abs(g) == 6:
            h = 0 if g > 0 else 1
            half = feat.at[at(-g), :, pl.ds(256 * h, 256)]
            rc(half, half, fn_s.at[1 + h], fn_r.at[5 + h], zp(2 if g > 0 else -2))
        rc(c, c, fn_s.at[0], fn_r.at[slot[g]], zp(1))
        rc(c, c, fn_s.at[0], fn_r.at[slot[g]], zp(-1))

    forward(0)

    loc_wf.wait()
    c_wf.wait_recv()
    wait_arrival(sc_buf.at[pl.ds(1, 15)], sc_r.at[0])

    def draft_send(o):
        rc(d_snd.at[o], d_rcv.at[o], xr_s.at[0], xr_r.at[0], xyp(-(o // 4), -lax.rem(o, 4)))

    def project(deltas):
        f = jnp.concatenate([feat[at(d)] for d in deltas], axis=0)
        y = jnp.dot(f[:, 0:256], wf[0], preferred_element_type=f32)
        y = y + jnp.dot(f[:, 256:512], wf[1], preferred_element_type=f32)
        for i, d in enumerate(deltas):
            o = at(d)
            scale = jnp.sum(jnp.where(eye, sc_buf[o], 0.0), axis=1, keepdims=True)
            out = y[32 * i : 32 * i + 32] * scale + q_buf[o]
            q_buf[o] = out
            d_snd[o] = out.astype(bf16)
            pl.when(o != 0)(functools.partial(draft_send, o))

    for g in (3, -3):
        i = slot[g]
        f_far[g].wait_recv()
        forward(g)
    loc_we.wait()
    c_we.wait_recv()
    wait_arrival(em.at[pl.ds(0, 10)], en_r.at[0])
    wait_arrival(em.at[0, 0], en_r.at[1])
    wait_arrival(em.at[0, 1], en_r.at[2])
    for a in range(4):
        es = [em[lax.rem(cx + (4 - a), 4) * 4 + lax.rem(cy + (4 - b), 4)] for b in range(4)]
        q = 0.0
        for h in range(2):
            e = jnp.concatenate([v[h] for v in es], axis=0)
            q = q + jnp.dot(e, we[h], preferred_element_type=f32)
        q_buf[4 * a : 4 * a + 4] = q.reshape(4, 32, 512)
    for g in (6, -6):
        i = slot[g]
        f_far[g].wait_recv()
        forward(g)
    for g, deltas in (
        (0, (-1, 0, 1)), (3, (-4, -3, -2)), (-3, (2, 3, 4)), (6, (-7, -6, -5)), (-6, (5, 6, 7, 8))
    ):
        i = slot[g]
        wait_arrival(feat.at[pl.ds(0, 2)], fn_r.at[i])
        if g == -6:
            wait_arrival(feat.at[0, :, pl.ds(0, 256)], fn_r.at[5])
            wait_arrival(feat.at[0, :, pl.ds(256, 256)], fn_r.at[6])
        project(deltas)

    wait_arrival(d_rcv.at[pl.ds(1, 15)], xr_r.at[0])
    mine = q_buf[0]
    for o in range(1, 16):
        mine = mine + d_rcv[o].astype(f32)
    mine = mine.reshape(4, 8, 512)
    for r in range(4):
        draft_ref[r] = jnp.where(t3[r] <= acc_ref[r], mine[r], 0.0).astype(bf16)
    draft_out = pltpu.make_async_copy(draft_ref, draft_hbm, loc_sem.at[16])
    draft_out.start()
    ns_out.wait()
    for c in (c_em, c_wo, c_we, c_wf):
        c.wait_send()
    chunk_half = feat.at[0, :, pl.ds(0, 256)]
    wait_leave(g_buf.at[pl.ds(1, 15)], ag_s.at[0])
    wait_leave(em.at[pl.ds(0, 4)], ez_s.at[0])
    wait_leave(em.at[pl.ds(0, 10)], en_s.at[0])
    wait_leave(ssq_rcv.at[pl.ds(1, 15)], sq_s.at[0])
    wait_leave(sc_buf.at[pl.ds(1, 15)], sc_s.at[0])
    wait_leave(feat.at[pl.ds(0, 10)], rs_s.at[0])
    wait_leave(r2, rf_s.at[0])
    wait_leave(feat.at[pl.ds(0, 4)], ff_s.at[0])
    wait_leave(feat.at[pl.ds(0, 10)], fn_s.at[0])
    wait_leave(d_rcv.at[pl.ds(1, 15)], xr_s.at[0])
    for sems in (en_s, rs_s, fn_s):
        wait_leave(chunk_half, sems.at[1])
        wait_leave(chunk_half, sems.at[2])
    draft_out.wait()


def finish(draft_in, ns_in, draft_out, ns_out, draft_v, ns_v, sem):
    def moves(i):
        if i == 4:
            return (draft_in, draft_v, sem.at[4]), (draft_v, draft_out, sem.at[9])
        return (ns_in.at[i], ns_v.at[i], sem.at[i]), (ns_v.at[i], ns_out.at[i], sem.at[5 + i])

    arrive = [pltpu.make_async_copy(*moves(i)[0]) for i in range(5)]
    leave = [pltpu.make_async_copy(*moves(i)[1]) for i in range(5)]
    for c in arrive:
        c.start()
    for c, d in zip(arrive, leave):
        c.wait()
        d.start()
    for d in leave:
        d.wait()


def body(
    ssm_input, gate_input, write_vectors, read_vectors, step_logit, step_bias, decay_rate, skip_gain,
    norm_gain, ssm_state, accepted, out_weight, token_embeds, feat_weight, embed_weight,
):
    hbm = pl.BlockSpec(memory_space=pltpu.HBM)
    dma = pltpu.SemaphoreType.DMA
    draft, new_state = pl.pallas_call(
        kernel,
        out_shape=(
            jax.ShapeDtypeStruct((4, 8, 512), bf16),
            jax.ShapeDtypeStruct((4, 512, 256), bf16),
        ),
        in_specs=[hbm] * 15,
        out_specs=(hbm, hbm),
        scratch_shapes=[
            pltpu.VMEM((4, 8, 512), bf16),
            pltpu.VMEM((4, 8, 512), bf16),
            pltpu.VMEM((4, 8, 256), bf16),
            pltpu.VMEM((4, 8, 256), bf16),
            pltpu.VMEM((4, 8, 8), f32),
            pltpu.SMEM((8,), f32),
            pltpu.SMEM((8,), f32),
            pltpu.SMEM((8,), f32),
            pltpu.VMEM((512,), f32),
            pltpu.SMEM((4,), jnp.int32),
            pltpu.VMEM((8, 8, 256), bf16),
            pltpu.VMEM((4, 8, 512), bf16),
            pltpu.VMEM((4, 512, 256), bf16),
            pltpu.VMEM((4, 512, 256), bf16),
            pltpu.VMEM((2, 512, 256), bf16),
            pltpu.VMEM((2, 256, 512), bf16),
            pltpu.VMEM((2, 256, 512), bf16),
            pltpu.VMEM((2, 32, 256), bf16),
            pltpu.VMEM((16, 2, 32, 256), bf16),
            pltpu.VMEM((16, 32, 512), bf16),
            pltpu.VMEM((5, 32, 512), f32),
            pltpu.VMEM((5, 4, 32, 512), bf16),
            pltpu.VMEM((5, 3, 32, 512), bf16),
            pltpu.VMEM((4, 32, 512), bf16),
            pltpu.VMEM((4, 32, 512), bf16),
            pltpu.VMEM((16, 32, 512), bf16),
            pltpu.VMEM((16, 32, 512), f32),
            pltpu.VMEM((16, 32, 512), bf16),
            pltpu.VMEM((16, 32, 512), bf16),
            pltpu.VMEM((1, 128), f32),
            pltpu.VMEM((16, 1, 128), f32),
            pltpu.VMEM((16, 1, 128), f32),
            dma((17,)),
            dma((4,)), dma((4,)),
            dma((1,)), dma((1,)),
            dma((3,)), dma((3,)),
            dma((1,)), dma((5,)),
            dma((1,)), dma((1,)),
            dma((1,)), dma((1,)),
            dma((3,)), dma((7,)),
            dma((1,)), dma((1,)),
            dma((1,)), dma((4,)),
            dma((3,)), dma((7,)),
            dma((1,)), dma((1,)),
        ],
        compiler_params=pltpu.CompilerParams(
            collective_id=0, has_side_effects=True, vmem_limit_bytes=56 * 1024 * 1024
        ),
        name="verify_step",
    )(
        ssm_input, gate_input, write_vectors, read_vectors, step_logit, step_bias, decay_rate, skip_gain,
        norm_gain, ssm_state.reshape(4, 512, 256), accepted, out_weight, token_embeds, feat_weight, embed_weight,
    )
    draft, new_state = pl.pallas_call(
        finish,
        out_shape=(
            jax.ShapeDtypeStruct((4, 8, 512), bf16),
            jax.ShapeDtypeStruct((4, 512, 256), bf16),
        ),
        in_specs=[hbm] * 2,
        out_specs=(hbm, hbm),
        scratch_shapes=[pltpu.VMEM((4, 8, 512), bf16), pltpu.VMEM((4, 512, 256), bf16), dma((10,))],
        name="results",
    )(draft, new_state)
    return draft, new_state.reshape(4, 8, 64, 256)


def solution(mesh):
    in_specs = (
        P("row", None, "tensor"),
        P("row", None, "tensor"),
        P("row", None, "tensor"),
        P("row", None, "tensor"),
        P("row", None, "tensor"),
        P("tensor"),
        P("tensor"),
        P("tensor"),
        P("tensor"),
        P("row", "tensor", None, None),
        P("row"),
        P("tensor", "row"),
        P("tensor", None, "row"),
        P("row", "tensor"),
        P("row", "tensor"),
    )
    out_specs = (P("row", None, "tensor"), P("row", "tensor", None, None))
    return jax.shard_map(body, mesh=mesh, in_specs=in_specs, out_specs=out_specs, check_vma=False)
```

time: 87.5 us -> 62.7 us (0.72)
  the two profiles are of different devices: /device:TPU:36 before, /device:TPU:6 now
where the time goes in v2:
time: 62.7 us; the launch traced here: 62.5 us
  Pallas kernels  61.9 us (99%)
  between operations  0.64 us (1%)
    pallas_call x1, Pallas kernels, body(): pl.pallas_call(kernel, out_shape=(jax.ShapeDtypeStruct((4, 8, 512), bf16)...  59.9 us
    pallas_call x1, Pallas kernels, body(): pl.pallas_call(finish, out_shape=(jax.ShapeDtypeStruct((4, 8, 512), bf16)...  2 us

profile of v2, /device:TPU:6, one launch (start us, length us, event | category | flops | bytes accessed | tf_op | source)
XLA Modules:
  0.0 62.5 jit_solution(17540907073994547568)
XLA Ops:
  0.6 59.9 %verify_step.1 = (bf16[4,8,512]{2,1,0:T(8,128)(2,1)}, bf16[4,512,256]{2,1,0:T(8,128)(2,1)}) custom-call(bf16[4,8,512]{2,1,0:T(8,128)(2,1)} %x_hbm.1, bf16[4,8,512]{2,1,0:T(8,128)(2,1)} %gate_hbm.1, bf16[4,8,256]{2,1,0:T(8,128)(2,1)} %b_hbm.1, bf16[4,8,256]{2,1,0:T(8,128)(2,1)} %c_hbm.1, f32[4,8,8]{2,1,0:T(8,128)} %logit_hbm.1, f32[8]{0:T(128)} %bias_hbm.1, ...), custom_call_target="tpu_custom_call" | custom-call | tf_op jit(solution)/shard_map/verify_step/pallas_call | solution.py:357
  60.5 2.0 %results.1 = (bf16[4,8,512]{2,1,0:T(8,128)(2,1)}, bf16[4,512,256]{2,1,0:T(8,128)(2,1)}) custom-call(bf16[4,8,512]{2,1,0:T(8,128)(2,1)} %get-tuple-element.6.draft_in, bf16[4,512,256]{2,1,0:T(8,128)(2,1)} %get-tuple-element.7.ns_in), custom_call_target="tpu_custom_call" | custom-call | tf_op jit(solution)/shard_map/results/pallas_call | solution.py:419

commit v3 on v2

--- a/solution.py
+++ b/solution.py
@@ -29,8 +29,8 @@
     draft_hbm, ns_hbm,
     x_ref, gate_ref, b_ref, c_ref, logit_ref, bias_ref, decay_ref, skip_ref, gain_ref, acc_ref, emb_ref,
     draft_ref, ns_ref, state_v, wo, wf, we, em_own, em, g_buf, p_own, p_snd, r1, s_snd, r2, feat, q_buf, d_snd, d_rcv,
-    ssq_own, ssq_rcv, sc_buf,
-    loc_sem, sib_s, sib_r, ez_s, ez_r, en_s, en_r, ag_s, ag_r, sq_s, sq_r, sc_s, sc_r, rs_s, rs_r,
+    ssq_own, ssq_snd, ssq_rcv, sc_buf,
+    past_sem, loc_sem, sib_s, sib_r, ez_s, ez_r, en_s, en_r, ag_s, ag_r, sq_s, sq_r, sc_s, sc_r, rs_s, rs_r,
     rf_s, rf_r, ff_s, ff_r, fn_s, fn_r, xr_s, xr_r,
 ):
     groups = (6, -6, 3, -3, 0)
@@ -52,9 +52,14 @@
     def xyp(dx, dy):
         return ((lax.rem(cx + (dx + 4), 4) * 4 + lax.rem(cy + (dy + 4), 4)) * 2 + core, z)
 
+    def place(o):
+        p = lax.rem(5 * o, 16)
+        return p // 4, lax.rem(p, 4)
+
     xy_all = [(a, b) for a in range(4) for b in range(4) if (a, b) != (0, 0)]
     barrier = pltpu.get_barrier_semaphore()
-    peers = [sib] + [(sib[0], at(d)) for d in (6, -6, 3, -3)] + [zp(d) for d in range(1, 16)] + [xyp(a, b) for a, b in xy_all]
+    peers = [xyp(a, b) for a, b in sorted(xy_all, key=lambda p: -min(p[0], 4 - p[0]) - min(p[1], 4 - p[1]))]
+    peers += [zp(3), zp(-3), (sib[0], at(3)), (sib[0], at(-3)), zp(2), zp(-2), zp(1), zp(-1), sib]
     for p in peers:
         pl.semaphore_signal(barrier, inc=1, device_id=p, device_id_type=MESH)
 
@@ -140,7 +145,8 @@
 
     pl.semaphore_wait(barrier, len(peers))
     def normed_send(o, i):
-        rc(g_buf.at[0], g_buf.at[o], ag_s.at[0], ag_r.at[i], xyp(o // 4, lax.rem(o, 4)))
+        dx, dy = place(o)
+        rc(g_buf.at[0], g_buf.at[o], ag_s.at[0], ag_r.at[i], xyp(dx, dy))
 
     members = {g: (-1, 0, 1, 2) if g == 6 else (-1, 0, 1) for g in groups}
     for g in groups:
@@ -152,9 +158,13 @@
     c_we = rc(we_hbm, we.at[1], sib_s.at[2], sib_r.at[2], sib)
     c_wf = rc(wf_hbm, wf.at[1], sib_s.at[3], sib_r.at[3], sib)
 
-    for g in (6, -6, 3, -3):
+    def embeds_far(g):
         rc(em_own.at[core], em.at[z, 0], ez_s.at[0], ez_r.at[0], zp(g))
         rc(em_own.at[1 - core], em.at[z, 1], ez_s.at[0], ez_r.at[0], (sib[0], at(g)))
+
+    for g in (3, -3):
+        pl.semaphore_signal(past_sem, inc=1, device_id=zp(g), device_id_type=MESH)
+        embeds_far(g)
 
     def embeds_near(g):
         o = at(-g)
@@ -165,8 +175,8 @@
         rc(em.at[o], em.at[o], en_s.at[0], en_r.at[0], zp(1))
         rc(em.at[o], em.at[o], en_s.at[0], en_r.at[0], zp(-1))
 
-    for d in range(1, 16):
-        rc(ssq_own, ssq_rcv.at[d], sq_s.at[0], sq_r.at[0], zp(d))
+    for i, d in enumerate((1, -1, -2)):
+        rc(ssq_own, ssq_rcv.at[i], sq_s.at[0], sq_r.at[0], zp(d))
     c_em.wait_recv()
     embeds_near(0)
 
@@ -186,6 +196,10 @@
     ns_out = pltpu.make_async_copy(ns_ref, ns_hbm, loc_sem.at[15])
     ns_out.start()
 
+    pl.semaphore_wait(past_sem, 2)
+    for g in (6, -6):
+        embeds_far(g)
+
     loc_wo.wait()
     c_wo.wait_recv()
     for g in groups:
@@ -200,16 +214,25 @@
             cols = pl.ds(256 * h, 256)
             p_own[i, :, cols] = part[1]
             p_snd[i, 0:n, :, cols] = part.astype(bf16)
+        if g == 6:
+            for j in range(2):
+                cols = pl.ds(256 * j, 256)
+                rc(p_snd.at[0, 3, :, cols], r1.at[j, 2, :, cols], rs_s.at[1 + j], rs_r.at[5 + j], zp(2 - 4 * j))
         rc(p_snd.at[i, 2], r1.at[i, 0], rs_s.at[0], rs_r.at[i], zp(1))
         rc(p_snd.at[i, 0], r1.at[i, 1], rs_s.at[0], rs_r.at[i], zp(-1))
-        if g == 6:
-            cols = pl.ds(0, 256)
-            rc(p_snd.at[0, 3, :, cols], r1.at[i, 2, :, cols], rs_s.at[1], rs_r.at[5], zp(2))
-        if g == -6:
-            cols = pl.ds(256, 256)
-            rc(p_snd.at[0, 3, :, cols], r1.at[i, 2, :, cols], rs_s.at[2], rs_r.at[6], zp(-2))
+
+    wait_arrival(ssq_rcv.at[pl.ds(0, 3)], sq_r.at[0])
+    window = ssq_own[...] + ssq_rcv[0] + ssq_rcv[1]
+    ssq_snd[0] = window
+    ssq_snd[1] = window + ssq_rcv[2]
+    for i, d in enumerate((3, -3, 6, -6)):
+        rc(ssq_snd.at[1 if d == -6 else 0], ssq_rcv.at[3 + i], sq_s.at[1], sq_r.at[1], zp(d))
 
     for g in groups:
+        if g == 0:
+            wait_arrival(em.at[pl.ds(0, 4)], ez_r.at[0])
+            for e in (6, -6, 3, -3):
+                embeds_near(e)
         i = slot[g]
         wait_arrival(r1.at[i, pl.ds(0, 2)], rs_r.at[i])
         p_own[i] = p_own[i] + r1[i, 0].astype(f32) + r1[i, 1].astype(f32)
@@ -219,27 +242,16 @@
             p_own[i, :, cols] = p_own[i, :, cols] + r1[i, 2, :, cols].astype(f32)
         if g != 0:
             s_snd[i] = p_own[i].astype(bf16)
-            rc(s_snd.at[i], r2.at[i], rf_s.at[0], rf_r.at[0], zp(g))
-
-    wait_arrival(em.at[pl.ds(0, 4)], ez_r.at[0])
-    for g in (6, -6, 3, -3):
-        embeds_near(g)
-
-    total = ssq_own[...]
-    wait_arrival(ssq_rcv.at[pl.ds(1, 15)], sq_r.at[0])
-    for d in range(1, 16):
-        total = total + ssq_rcv[d]
-    sc_buf[0] = lax.rsqrt(total / 8192.0 + norm_eps)
-    for a, b in xy_all:
-        rc(sc_buf.at[0], sc_buf.at[a * 4 + b], sc_s.at[0], sc_r.at[0], xyp(a, b))
-
-    wait_arrival(r2, rf_r.at[0])
+            rc(s_snd.at[i], r2.at[i], rf_s.at[0], rf_r.at[i // 2], zp(g))
+
+    wait_arrival(r2.at[pl.ds(2, 2)], rf_r.at[1])
+    wait_arrival(r2.at[pl.ds(0, 2)], rf_r.at[0])
     total = p_own[slot[0]]
     for g in (3, -3, 6, -6):
         total = total + r2[slot[g]].astype(f32)
     feat[z] = total.astype(bf16)
     f_far = {}
-    for g in (6, -6, 3, -3):
+    for g in (3, -3, 6, -6):
         f_far[g] = rc(feat.at[z], feat.at[z], ff_s.at[0], ff_r.at[slot[g]], zp(g))
 
     def forward(g):
@@ -253,17 +265,22 @@
 
     forward(0)
 
+    wait_arrival(ssq_rcv.at[pl.ds(3, 4)], sq_r.at[1])
+    total = ssq_snd[0] + ssq_rcv[3] + ssq_rcv[4] + ssq_rcv[5] + ssq_rcv[6]
+    sc_buf[0] = lax.rsqrt(total / 8192.0 + norm_eps)
+    for o in range(1, 16):
+        rc(sc_buf.at[0], sc_buf.at[o], sc_s.at[0], sc_r.at[0], xyp(5 * o % 16 // 4, 5 * o % 4))
+
     loc_wf.wait()
     c_wf.wait_recv()
-    wait_arrival(sc_buf.at[pl.ds(1, 15)], sc_r.at[0])
 
     def draft_send(o):
-        rc(d_snd.at[o], d_rcv.at[o], xr_s.at[0], xr_r.at[0], xyp(-(o // 4), -lax.rem(o, 4)))
+        dx, dy = place(o)
+        rc(d_snd.at[o], d_rcv.at[o], xr_s.at[0], xr_r.at[0], xyp(-dx, -dy))
 
     def project(deltas):
         f = jnp.concatenate([feat[at(d)] for d in deltas], axis=0)
-        y = jnp.dot(f[:, 0:256], wf[0], preferred_element_type=f32)
-        y = y + jnp.dot(f[:, 256:512], wf[1], preferred_element_type=f32)
+        y = jnp.dot(f, wf[...].reshape(512, 512), preferred_element_type=f32)
         for i, d in enumerate(deltas):
             o = at(d)
             scale = jnp.sum(jnp.where(eye, sc_buf[o], 0.0), axis=1, keepdims=True)
@@ -276,13 +293,17 @@
         i = slot[g]
         f_far[g].wait_recv()
         forward(g)
+    wait_arrival(sc_buf.at[pl.ds(1, 15)], sc_r.at[0])
     loc_we.wait()
     c_we.wait_recv()
     wait_arrival(em.at[pl.ds(0, 10)], en_r.at[0])
     wait_arrival(em.at[0, 0], en_r.at[1])
     wait_arrival(em.at[0, 1], en_r.at[2])
     for a in range(4):
-        es = [em[lax.rem(cx + (4 - a), 4) * 4 + lax.rem(cy + (4 - b), 4)] for b in range(4)]
+        es = []
+        for o in range(4 * a, 4 * a + 4):
+            dx, dy = 5 * o % 16 // 4, 5 * o % 4
+            es.append(em[lax.rem(cx + (4 - dx), 4) * 4 + lax.rem(cy + (4 - dy), 4)])
         q = 0.0
         for h in range(2):
             e = jnp.concatenate([v[h] for v in es], axis=0)
@@ -318,7 +339,8 @@
     wait_leave(g_buf.at[pl.ds(1, 15)], ag_s.at[0])
     wait_leave(em.at[pl.ds(0, 4)], ez_s.at[0])
     wait_leave(em.at[pl.ds(0, 10)], en_s.at[0])
-    wait_leave(ssq_rcv.at[pl.ds(1, 15)], sq_s.at[0])
+    wait_leave(ssq_rcv.at[pl.ds(0, 3)], sq_s.at[0])
+    wait_leave(ssq_rcv.at[pl.ds(3, 4)], sq_s.at[1])
     wait_leave(sc_buf.at[pl.ds(1, 15)], sc_s.at[0])
     wait_leave(feat.at[pl.ds(0, 10)], rs_s.at[0])
     wait_leave(r2, rf_s.at[0])
@@ -393,17 +415,19 @@
             pltpu.VMEM((16, 32, 512), bf16),
             pltpu.VMEM((16, 32, 512), bf16),
             pltpu.VMEM((1, 128), f32),
+            pltpu.VMEM((2, 1, 128), f32),
+            pltpu.VMEM((7, 1, 128), f32),
             pltpu.VMEM((16, 1, 128), f32),
-            pltpu.VMEM((16, 1, 128), f32),
+            pltpu.SemaphoreType.REGULAR,
             dma((17,)),
             dma((4,)), dma((4,)),
             dma((1,)), dma((1,)),
             dma((3,)), dma((3,)),
             dma((1,)), dma((5,)),
-            dma((1,)), dma((1,)),
+            dma((2,)), dma((2,)),
             dma((1,)), dma((1,)),
             dma((3,)), dma((7,)),
-            dma((1,)), dma((1,)),
+            dma((1,)), dma((2,)),
             dma((1,)), dma((4,)),
             dma((3,)), dma((7,)),
             dma((1,)), dma((1,)),

time: 62.7 us -> 59.2 us (0.944); the launches traced: 62.5 us -> 58.4 us
  Pallas kernels: 61.9 us -> 57.7 us
    pallas_call x1, Pallas kernels: 59.9 us -> 55.7 us  [body(): pl.pallas_call(kernel, out_shape=(jax.ShapeDtypeStruct((4, 8, 512), bf16)...]
where the time goes in v3:
time: 59.2 us; the launch traced here: 58.4 us
  Pallas kernels  57.7 us (97%)
  between operations  0.64 us (1%)
    pallas_call x1, Pallas kernels, body(): pl.pallas_call(kernel, out_shape=(jax.ShapeDtypeStruct((4, 8, 512), bf16)...  55.7 us
    pallas_call x1, Pallas kernels, body(): pl.pallas_call(finish, out_shape=(jax.ShapeDtypeStruct((4, 8, 512), bf16)...  2 us

profile of v3, /device:TPU:6, one launch (start us, length us, event | category | flops | bytes accessed | tf_op | source)
XLA Modules:
  0.0 58.4 jit_solution(17946565509019801170)
XLA Ops:
  0.6 55.7 %verify_step.1 = (bf16[4,8,512]{2,1,0:T(8,128)(2,1)}, bf16[4,512,256]{2,1,0:T(8,128)(2,1)}) custom-call(bf16[4,8,512]{2,1,0:T(8,128)(2,1)} %x_hbm.1, bf16[4,8,512]{2,1,0:T(8,128)(2,1)} %gate_hbm.1, bf16[4,8,256]{2,1,0:T(8,128)(2,1)} %b_hbm.1, bf16[4,8,256]{2,1,0:T(8,128)(2,1)} %c_hbm.1, f32[4,8,8]{2,1,0:T(8,128)} %logit_hbm.1, f32[8]{0:T(128)} %bias_hbm.1, ...), custom_call_target="tpu_custom_call" | custom-call | tf_op jit(solution)/shard_map/verify_step/pallas_call | solution.py:379
  56.4 2.0 %results.1 = (bf16[4,8,512]{2,1,0:T(8,128)(2,1)}, bf16[4,512,256]{2,1,0:T(8,128)(2,1)}) custom-call(bf16[4,8,512]{2,1,0:T(8,128)(2,1)} %get-tuple-element.6.draft_in, bf16[4,512,256]{2,1,0:T(8,128)(2,1)} %get-tuple-element.7.ns_in), custom_call_target="tpu_custom_call" | custom-call | tf_op jit(solution)/shard_map/results/pallas_call | solution.py:443

commit v4 on v3

--- a/solution.py
+++ b/solution.py
@@ -251,7 +251,7 @@
         total = total + r2[slot[g]].astype(f32)
     feat[z] = total.astype(bf16)
     f_far = {}
-    for g in (3, -3, 6, -6):
+    for g in (6, -6, 3, -3):
         f_far[g] = rc(feat.at[z], feat.at[z], ff_s.at[0], ff_r.at[slot[g]], zp(g))
 
     def forward(g):

time: 59.2 us -> 58.9 us (level)
  no operation moved by 1% of the time
where the time goes in v4:
time: 58.9 us; the launch traced here: 57.9 us
  Pallas kernels  57.2 us (97%)
  between operations  0.64 us (1%)
    pallas_call x1, Pallas kernels, body(): pl.pallas_call(kernel, out_shape=(jax.ShapeDtypeStruct((4, 8, 512), bf16)...  55.2 us
    pallas_call x1, Pallas kernels, body(): pl.pallas_call(finish, out_shape=(jax.ShapeDtypeStruct((4, 8, 512), bf16)...  2 us

profile of v4, /device:TPU:6, one launch (start us, length us, event | category | flops | bytes accessed | tf_op | source)
XLA Modules:
  0.0 57.9 jit_solution(7477340468177357030)
XLA Ops:
  0.6 55.2 %verify_step.1 = (bf16[4,8,512]{2,1,0:T(8,128)(2,1)}, bf16[4,512,256]{2,1,0:T(8,128)(2,1)}) custom-call(bf16[4,8,512]{2,1,0:T(8,128)(2,1)} %x_hbm.1, bf16[4,8,512]{2,1,0:T(8,128)(2,1)} %gate_hbm.1, bf16[4,8,256]{2,1,0:T(8,128)(2,1)} %b_hbm.1, bf16[4,8,256]{2,1,0:T(8,128)(2,1)} %c_hbm.1, f32[4,8,8]{2,1,0:T(8,128)} %logit_hbm.1, f32[8]{0:T(128)} %bias_hbm.1, ...), custom_call_target="tpu_custom_call" | custom-call | tf_op jit(solution)/shard_map/verify_step/pallas_call | solution.py:379
  55.9 2.0 %results.1 = (bf16[4,8,512]{2,1,0:T(8,128)(2,1)}, bf16[4,512,256]{2,1,0:T(8,128)(2,1)}) custom-call(bf16[4,8,512]{2,1,0:T(8,128)(2,1)} %get-tuple-element.6.draft_in, bf16[4,512,256]{2,1,0:T(8,128)(2,1)} %get-tuple-element.7.ns_in), custom_call_target="tpu_custom_call" | custom-call | tf_op jit(solution)/shard_map/results/pallas_call | solution.py:443

commit v5 on v4

--- a/solution.py
+++ b/solution.py
@@ -274,11 +274,13 @@
     loc_wf.wait()
     c_wf.wait_recv()
 
-    def draft_send(o):
+    def draft_send(o, part):
         dx, dy = place(o)
-        rc(d_snd.at[o], d_rcv.at[o], xr_s.at[0], xr_r.at[0], xyp(-dx, -dy))
-
-    def project(deltas):
+        rc(d_snd.at[o], d_rcv.at[o], xr_s.at[0], xr_r.at[part], xyp(-dx, -dy))
+
+    d_rcv[0] = jnp.zeros((32, 512), bf16)
+
+    def project(deltas, part):
         f = jnp.concatenate([feat[at(d)] for d in deltas], axis=0)
         y = jnp.dot(f, wf[...].reshape(512, 512), preferred_element_type=f32)
         for i, d in enumerate(deltas):
@@ -287,7 +289,7 @@
             out = y[32 * i : 32 * i + 32] * scale + q_buf[o]
             q_buf[o] = out
             d_snd[o] = out.astype(bf16)
-            pl.when(o != 0)(functools.partial(draft_send, o))
+            pl.when(o != 0)(functools.partial(draft_send, o, part))
 
     for g in (3, -3):
         i = slot[g]
@@ -321,12 +323,18 @@
         if g == -6:
             wait_arrival(feat.at[0, :, pl.ds(0, 256)], fn_r.at[5])
             wait_arrival(feat.at[0, :, pl.ds(256, 256)], fn_r.at[6])
-        project(deltas)
-
-    wait_arrival(d_rcv.at[pl.ds(1, 15)], xr_r.at[0])
-    mine = q_buf[0]
-    for o in range(1, 16):
-        mine = mine + d_rcv[o].astype(f32)
+        project(deltas, 1 if abs(g) == 6 else 0)
+
+    parts = ((0, -1, 1, -2, 2, -3, 3, -4, 4), (5, 6, 7, 8, -5, -6, -7))
+    mine = 0.0
+    for j, deltas in enumerate(parts):
+        n = len(deltas)
+        own_inside = functools.reduce(jnp.logical_or, [at(d) == 0 for d in deltas])
+        pl.when(own_inside)(lambda n=n, j=j: wait_arrival(d_rcv.at[pl.ds(1, n - 1)], xr_r.at[j]))
+        pl.when(jnp.logical_not(own_inside))(lambda n=n, j=j: wait_arrival(d_rcv.at[pl.ds(1, n)], xr_r.at[j]))
+        for d in deltas:
+            mine = mine + d_rcv[at(d)].astype(f32)
+    mine = mine + q_buf[0]
     mine = mine.reshape(4, 8, 512)
     for r in range(4):
         draft_ref[r] = jnp.where(t3[r] <= acc_ref[r], mine[r], 0.0).astype(bf16)
@@ -430,7 +438,7 @@
             dma((1,)), dma((2,)),
             dma((1,)), dma((4,)),
             dma((3,)), dma((7,)),
-            dma((1,)), dma((1,)),
+            dma((1,)), dma((2,)),
         ],
         compiler_params=pltpu.CompilerParams(
             collective_id=0, has_side_effects=True, vmem_limit_bytes=56 * 1024 * 1024

time: 58.9 us -> 58.9 us (level)
  no operation moved by 1% of the time
where the time goes in v5:
time: 58.9 us; the launch traced here: 57.9 us
  Pallas kernels  57.2 us (97%)
  between operations  0.64 us (1%)
    pallas_call x1, Pallas kernels, body(): pl.pallas_call(kernel, out_shape=(jax.ShapeDtypeStruct((4, 8, 512), bf16)...  55.2 us
    pallas_call x1, Pallas kernels, body(): pl.pallas_call(finish, out_shape=(jax.ShapeDtypeStruct((4, 8, 512), bf16)...  2 us

profile of v5, /device:TPU:6, one launch (start us, length us, event | category | flops | bytes accessed | tf_op | source)
XLA Modules:
  0.0 57.9 jit_solution(3184966680888459156)
XLA Ops:
  0.6 55.2 %verify_step.1 = (bf16[4,8,512]{2,1,0:T(8,128)(2,1)}, bf16[4,512,256]{2,1,0:T(8,128)(2,1)}) custom-call(bf16[4,8,512]{2,1,0:T(8,128)(2,1)} %x_hbm.1, bf16[4,8,512]{2,1,0:T(8,128)(2,1)} %gate_hbm.1, bf16[4,8,256]{2,1,0:T(8,128)(2,1)} %b_hbm.1, bf16[4,8,256]{2,1,0:T(8,128)(2,1)} %c_hbm.1, f32[4,8,8]{2,1,0:T(8,128)} %logit_hbm.1, f32[8]{0:T(128)} %bias_hbm.1, ...), custom_call_target="tpu_custom_call" | custom-call | tf_op jit(solution)/shard_map/verify_step/pallas_call | solution.py:387
  55.9 2.0 %results.1 = (bf16[4,8,512]{2,1,0:T(8,128)(2,1)}, bf16[4,512,256]{2,1,0:T(8,128)(2,1)}) custom-call(bf16[4,8,512]{2,1,0:T(8,128)(2,1)} %get-tuple-element.6.draft_in, bf16[4,512,256]{2,1,0:T(8,128)(2,1)} %get-tuple-element.7.ns_in), custom_call_target="tpu_custom_call" | custom-call | tf_op jit(solution)/shard_map/results/pallas_call | solution.py:451
